TPU v7x, 32 devices: a whole 2x2x4 slice. The times are simulated.
32 devices in a mesh: view: 4 (over y, core), wide: 8 (over z, x).
Axes of the slice: x: 2, y: 2, z: 4, core: 2. Of those that a mesh axis runs over, the one named last changes fastest.
Arguments:
- splats: float32 [7, 262144], P(None, 'wide'), may hold values from -3 to 1024, as said below
- camera: float32 [4, 6], P('view'), may hold values from -2 to 2, as said below
- column_perm: int32 [4, 8, 32], P('view', None, 'wide'), may hold values from 0 to 31, as said below
- block_lists: int32 [4, 8, 32, 4], P('view', None, 'wide'), may hold values from 0 to 2047, as said below
- list_lengths: int32 [4, 8, 32], P('view', None, 'wide'), may hold values from 1 to 4, 64 in all within a row
- target: float32 [4, 3, 256, 1024], P('view', None, 'wide'), may hold values from 0.1 to 1
Outputs:
- rendered: float32 [4, 3, 256, 1024], P('view', None, 'wide')
- splat_grads: float32 [7, 262144], P(None, 'wide')
Inputs may be any that keep to these rules, and one draw needn't show every extreme that they name: `column_perm`: each [v, r, :] is a permutation of 0 .. 31. `block_lists`: entry [v, r, s, k] = h * 256 + r * 32 + column_perm[v, r, s] for a holder h in 0 .. 7; the holders of one tile's list differ; the list entries held by one device name each holder exactly 16 times. `splats`: splat j belongs to block j // 128; its centre lies inside tile t = (j // 128) % 256 of the screen, t = 32 row + column. Log-scales lie in [log 0.7, log 2], opacity logits in [-3, 2], colours in [0, 1]. `camera`: A00 and A11 lie in [0.998, 1.002], A01 and A10 in [-0.002, 0.002], b0 and b1 in [-2, 2].
All inputs are finite; a program needn't handle non-finite values. No bound on the sum of `list_lengths` on one device may be relied on, other than what follows from the above.
Results may differ from a plain program's by a relative error of at most 0.0045.
Values may be sent and summed in bfloat16 or wider, within the bound.
A program may use at most 64 MiB of HBM per device.

v0:
```python
import functools
import math

import jax
import jax.numpy as jnp
from jax import lax
from jax.experimental import pallas as pl
from jax.experimental.pallas import tpu as pltpu
from jax.sharding import PartitionSpec as P

TILE = 32
BLOCK = 128
HALF = 5


first_const = 0.0001
second_const = 0.0009
blur_sigma = 1.5


def with_halo(array, sides, width):
    for axis, dim in sides:
        size, length = (lax.axis_size(axis), array.shape[dim])
        up = [(i, (i + 1) % size) for i in range(size - 1)]
        down = [(j, i) for i, j in up]
        last = lax.slice_in_dim(array, length - width, length, axis=dim)
        leading = lax.slice_in_dim(array, 0, width, axis=dim)
        before = lax.ppermute(last, axis, up)
        after = lax.ppermute(leading, axis, down)
        array = jnp.concatenate([before, array, after], axis=dim)
    return array


def project(raw_params, camera_matrix_row):
    pos_x = raw_params[..., 0, :]
    pos_y = raw_params[..., 1, :]
    screen_x = camera_matrix_row[0] * pos_x + camera_matrix_row[1] * pos_y + camera_matrix_row[4]
    screen_y = camera_matrix_row[2] * pos_x + camera_matrix_row[3] * pos_y + camera_matrix_row[5]
    precision_term = jnp.exp(-2.0 * raw_params[..., 2, :])
    opacity = jax.nn.sigmoid(raw_params[..., 3, :])
    return jnp.stack(
        [
            screen_x,
            screen_y,
            precision_term,
            opacity,
            raw_params[..., 4, :],
            raw_params[..., 5, :],
            raw_params[..., 6, :],
            jnp.zeros_like(pos_x),
        ],
        axis=-2,
    )


def conic_of(camera_matrix_row):
    first = (
        camera_matrix_row[0] * camera_matrix_row[0] + camera_matrix_row[1] * camera_matrix_row[1]
    )
    mixed = (
        camera_matrix_row[0] * camera_matrix_row[2] + camera_matrix_row[1] * camera_matrix_row[3]
    )
    second = (
        camera_matrix_row[2] * camera_matrix_row[2] + camera_matrix_row[3] * camera_matrix_row[3]
    )
    determinant = first * second - mixed * mixed
    return (second / determinant, -mixed / determinant, first / determinant)


CHUNK = 8
PIXELS = TILE * TILE
SPAN = CHUNK * TILE
LOG2E = math.log2(math.e)


def split_pair(values):
    high = values.astype(jnp.bfloat16)
    low = (values - high.astype(jnp.float32)).astype(jnp.bfloat16)
    return jnp.concatenate([high, low], axis=1)


def splat_rows(params, scalars, anchor_x, anchor_y):
    offset_x = params[0:1] - anchor_x
    offset_y = params[1:2] - anchor_y
    factor = (-0.5 * LOG2E) * params[2:3]
    across = lax.broadcasted_iota(jnp.int32, (TILE, BLOCK), 0).astype(jnp.float32) + 0.5
    delta_x = across - offset_x
    plane = (factor * scalars[0]) * delta_x * delta_x + jnp.log2(params[3:4])
    slope = (factor * (2.0 * scalars[1])) * delta_x
    bend = factor * scalars[2]
    return offset_y, delta_x, plane, slope, bend


def chunk_delta_y(offset_y, chunk):
    down = lax.broadcasted_iota(jnp.int32, (CHUNK, 1, BLOCK), 0).astype(jnp.float32)
    return down + (chunk * CHUNK + 0.5) - offset_y[None]


def chunk_coverage(delta_y, plane, slope, bend):
    exponent = plane[None] + delta_y * (slope[None] + bend[None] * delta_y)
    return jnp.exp2(exponent).reshape(SPAN, BLOCK)


def colour_halves(params):
    colours = params[4:8]
    high = colours.astype(jnp.bfloat16).astype(jnp.float32)
    return high, colours - high


def colour_rows(params):
    high, low = colour_halves(params)
    return jnp.concatenate(
        [high, low, high, jnp.zeros((4, BLOCK), jnp.float32)], axis=0
    ).astype(jnp.bfloat16)


def colour_columns(params, place):
    eight = jnp.concatenate(colour_halves(params), axis=0)
    lane_group = lax.broadcasted_iota(jnp.int32, (BLOCK, BLOCK), 0) // 8
    spread = jnp.where(lane_group == place, jnp.concatenate([eight] * (BLOCK // 8), axis=0), 0.0)
    columns = spread.T.astype(jnp.bfloat16)
    return jnp.concatenate([columns, columns], axis=0)


def draw_kernel(group, lengths, cols, rows, scalar_ref, blocks, before_mat, out, log_trans, acc):
    slot = pl.program_id(0)
    anchor_x = (cols[slot] * TILE).astype(jnp.float32)
    anchor_y = (rows[slot] * TILE).astype(jnp.float32)
    scalars = [scalar_ref[i] for i in range(3)]
    log_trans[...] = jnp.zeros_like(log_trans)
    place = lax.rem(slot, group)

    @pl.when(place == 0)
    def clear():
        acc[...] = jnp.zeros_like(acc)

    def layer(k, unused):
        params = blocks[0, k]
        offset_y, delta_x, plane, slope, bend = splat_rows(params, scalars, anchor_x, anchor_y)
        colours = colour_columns(params, place)
        for chunk in range(TILE // CHUNK):
            span = pl.ds(chunk * SPAN, SPAN)
            coverage = chunk_coverage(chunk_delta_y(offset_y, chunk), plane, slope, bend)
            sums = jnp.dot(
                split_pair(jnp.log(1.0 - coverage)),
                before_mat[...],
                preferred_element_type=jnp.float32,
            )
            weights = coverage * jnp.exp(log_trans[span] + sums[:, :BLOCK])
            log_trans[span] += sums[:, BLOCK:]
            acc[span] += jnp.dot(
                split_pair(weights), colours, preferred_element_type=jnp.float32
            )
        return unused

    lax.fori_loop(0, lengths[slot], layer, 0)

    @pl.when(place == group - 1)
    def finish():
        turned = acc[...].T[: 8 * group].reshape(group, 8, PIXELS)
        out[...] = turned[:, 0:3] + turned[:, 4:7]


def pull_kernel(
    lengths, cols, rows, scalar_ref, blocks, grads, before_mat, after_mat, out,
    carry, weight_store, ratio_store,
):
    slot = pl.program_id(0)
    length = lengths[slot]
    anchor_x = (cols[slot] * TILE).astype(jnp.float32)
    anchor_y = (rows[slot] * TILE).astype(jnp.float32)
    scalars = [scalar_ref[i] for i in range(7)]
    carry[...] = jnp.zeros_like(carry)
    out[...] = jnp.zeros_like(out)

    def layer(k, unused):
        params = blocks[0, k]
        offset_y, delta_x, plane, slope, bend = splat_rows(params, scalars, anchor_x, anchor_y)
        for chunk in range(TILE // CHUNK):
            span = pl.ds(chunk * SPAN, SPAN)
            coverage = chunk_coverage(chunk_delta_y(offset_y, chunk), plane, slope, bend)
            log_keep = jnp.log(1.0 - coverage)
            sums = jnp.dot(
                split_pair(log_keep), before_mat[...], preferred_element_type=jnp.float32
            )
            weight_store[k, span] = coverage * jnp.exp(carry[span] + sums[:, :BLOCK])
            ratio_store[k, span] = coverage * jnp.exp(-log_keep)
            carry[span] += sums[:, BLOCK:]
        return unused

    lax.fori_loop(0, length, layer, 0)
    carry[...] = jnp.zeros_like(carry)

    def back(step, unused):
        k = length - 1 - step
        params = blocks[0, k]
        offset_y, delta_x, plane, slope, bend = splat_rows(params, scalars, anchor_x, anchor_y)
        colours = colour_rows(params)
        zeros = jnp.zeros((TILE, BLOCK), jnp.float32)
        moment_0, moment_1, moment_2 = zeros, zeros, zeros
        colour_grads = jnp.zeros((16, BLOCK), jnp.float32)
        for chunk in range(TILE // CHUNK):
            span = pl.ds(chunk * SPAN, SPAN)
            delta_y = chunk_delta_y(offset_y, chunk)
            weights = weight_store[k, span]
            chunk_grads = grads[0, :, span]
            worth = lax.dot_general(
                chunk_grads,
                colours,
                (((0,), (0,)), ((), ())),
                preferred_element_type=jnp.float32,
            )
            shares = weights * worth
            sums = jnp.dot(
                split_pair(shares), after_mat[...], preferred_element_type=jnp.float32
            )
            behind = carry[span] + sums[:, :BLOCK]
            carry[span] += sums[:, BLOCK:]
            pull = (shares - behind * ratio_store[k, span]).reshape(CHUNK, TILE, BLOCK)
            tilted = pull * delta_y
            moment_0 += jnp.sum(pull, axis=0)
            moment_1 += jnp.sum(tilted, axis=0)
            moment_2 += jnp.sum(tilted * delta_y, axis=0)
            colour_grads += jnp.dot(
                chunk_grads, weights.astype(jnp.bfloat16), preferred_element_type=jnp.float32
            )
        qa, qb, qc, a00, a01, a10, a11 = scalars
        precision = params[2:3]
        leaned = delta_x * moment_0
        grad_u = precision * jnp.sum(qa * leaned + qb * moment_1, axis=0, keepdims=True)
        grad_w = precision * jnp.sum(qb * leaned + qc * moment_1, axis=0, keepdims=True)
        grad_s = precision * jnp.sum(
            delta_x * (qa * leaned + (2.0 * qb) * moment_1) + qc * moment_2, axis=0, keepdims=True
        )
        grad_o = (1.0 - params[3:4]) * jnp.sum(moment_0, axis=0, keepdims=True)
        out[0, k, 0:1] = a00 * grad_u + a10 * grad_w
        out[0, k, 1:2] = a01 * grad_u + a11 * grad_w
        out[0, k, 2:3] = grad_s
        out[0, k, 3:4] = grad_o
        out[0, k, 4:8] = colour_grads[0:4] + colour_grads[8:12]
        return unused

    lax.fori_loop(0, length, back, 0)


def triangle(after):
    row = jnp.arange(2 * BLOCK)[:, None] % BLOCK
    col = jnp.arange(2 * BLOCK)[None, :]
    inside = row > col if after else row < col
    return (inside | (col >= BLOCK)).astype(jnp.bfloat16)


def whole_spec(shape):
    return pl.BlockSpec(shape, lambda *unused: (0,) * len(shape))


def slot_spec(shape):
    return pl.BlockSpec((1,) + shape, lambda slot, *unused: (slot,) + (0,) * len(shape))


def draw_tiles(lengths, cols, rows, scalars, blocks):
    slots, depth = blocks.shape[0], blocks.shape[1]
    group = math.gcd(slots, BLOCK // 8)
    return pl.pallas_call(
        functools.partial(draw_kernel, group),
        grid_spec=pltpu.PrefetchScalarGridSpec(
            num_scalar_prefetch=4,
            grid=(slots,),
            in_specs=[slot_spec((depth, 8, BLOCK)), whole_spec((2 * BLOCK, 2 * BLOCK))],
            out_specs=pl.BlockSpec(
                (group, 3, PIXELS), lambda slot, *unused: (slot // group, 0, 0)
            ),
            scratch_shapes=[
                pltpu.VMEM((PIXELS, BLOCK), jnp.float32),
                pltpu.VMEM((PIXELS, BLOCK), jnp.float32),
            ],
        ),
        out_shape=jax.ShapeDtypeStruct((slots, 3, PIXELS), jnp.float32),
        compiler_params=pltpu.CompilerParams(vmem_limit_bytes=32 * 1024 * 1024),
    )(lengths, cols, rows, scalars, blocks, triangle(False))


def pull_tiles(lengths, cols, rows, scalars, blocks, grads):
    slots, depth = blocks.shape[0], blocks.shape[1]
    return pl.pallas_call(
        pull_kernel,
        grid_spec=pltpu.PrefetchScalarGridSpec(
            num_scalar_prefetch=4,
            grid=(slots,),
            in_specs=[
                slot_spec((depth, 8, BLOCK)),
                slot_spec((16, PIXELS)),
                whole_spec((2 * BLOCK, 2 * BLOCK)),
                whole_spec((2 * BLOCK, 2 * BLOCK)),
            ],
            out_specs=slot_spec((depth, 8, BLOCK)),
            scratch_shapes=[
                pltpu.VMEM((PIXELS, BLOCK), jnp.float32),
                pltpu.VMEM((depth, PIXELS, BLOCK), jnp.float32),
                pltpu.VMEM((depth, PIXELS, BLOCK), jnp.float32),
            ],
        ),
        out_shape=jax.ShapeDtypeStruct((slots, depth, 8, BLOCK), jnp.float32),
        compiler_params=pltpu.CompilerParams(vmem_limit_bytes=32 * 1024 * 1024),
    )(lengths, cols, rows, scalars, blocks, grads, triangle(False), triangle(True))


def blur_taps():
    raw_taps = [
        math.exp(-((offset - HALF) ** 2) / (2.0 * blur_sigma**2)) for offset in range(2 * HALF + 1)
    ]
    tap_total = sum(raw_taps)
    return [kernel_tap_value / tap_total for kernel_tap_value in raw_taps]


def blur_field(field, out_rows):
    tap_list = blur_taps()
    field_width = field.shape[2]
    padded_input = jnp.pad(field, ((0, 0), (0, 0), (HALF, HALF)))
    across = tap_list[0] * padded_input[:, :, 0:field_width]
    for offset in range(1, 2 * HALF + 1):
        across = across + tap_list[offset] * padded_input[:, :, offset : offset + field_width]
    result = tap_list[0] * across[:, 0:out_rows]
    for offset in range(1, 2 * HALF + 1):
        result = result + tap_list[offset] * across[:, offset : offset + out_rows]
    return result


def structure_loss(image_rows, target_rows, out_rows, row_weight, loss_scale):
    mean_image = blur_field(image_rows, out_rows)
    mean_target = blur_field(target_rows, out_rows)
    spread_image = blur_field(image_rows * image_rows, out_rows) - mean_image * mean_image
    spread_target = blur_field(target_rows * target_rows, out_rows) - mean_target * mean_target
    joint_spread = blur_field(image_rows * target_rows, out_rows) - mean_image * mean_target
    numerator = (2.0 * mean_image * mean_target + first_const) * (2.0 * joint_spread + second_const)
    denominator = (mean_image * mean_image + mean_target * mean_target + first_const) * (
        spread_image + spread_target + second_const
    )
    return jnp.sum(row_weight[None, :, None] * (1.0 - numerator / denominator)) / loss_scale


def add_views(partial):
    views = lax.axis_size("view")
    half = partial.shape[1] // 2
    odd = lax.rem(lax.axis_index("view"), 2) == 1
    mates = [(i, i ^ 1) for i in range(views)]
    left, right = partial[:, :half], partial[:, half:]
    theirs = lax.ppermute(jnp.where(odd, left, right), "view", mates)
    pair_sum = jnp.where(odd, right, left).astype(jnp.float32) + theirs.astype(jnp.float32)
    others = [
        lax.ppermute(pair_sum, "view", [(i, (i + 2 * step) % views) for i in range(views)])
        for step in range(1, views // 2)
    ]
    total = pair_sum
    for other in others:
        total = total + other
    mate_total = lax.ppermute(total, "view", mates)
    return jnp.concatenate(
        [jnp.where(odd, mate_total, total), jnp.where(odd, total, mate_total)], axis=1
    )


def on_device(splats, camera, column_perm, block_lists, list_lengths, target):
    wide_total = lax.axis_size("wide")
    view_total = lax.axis_size("view")
    camera_matrix_row = camera[0]
    conic_form = conic_of(camera_matrix_row)
    block_grand_total = splats.shape[1] // BLOCK
    stored = splats.reshape(7, block_grand_total, BLOCK).transpose(1, 0, 2)
    projected = project(stored, camera_matrix_row)
    row_total = column_perm.shape[1]
    per_row = column_perm.shape[2]
    slot_total = row_total * per_row
    list_depth = block_lists.shape[3]
    entries = block_lists.reshape(-1)
    entry_total = entries.shape[0]
    capacity = entry_total // wide_total
    holder = entries // block_grand_total
    local_ids = entries % block_grand_total
    owner_hits = (holder[:, None] == jnp.arange(wide_total, dtype=jnp.int32)[None, :]).astype(
        jnp.int32
    )
    bucket_rank = jnp.sum((jnp.cumsum(owner_hits, axis=0) - owner_hits) * owner_hits, axis=1)
    bucket_slot = holder * capacity + bucket_rank
    hits = (
        bucket_slot[:, None] == jnp.arange(entry_total, dtype=jnp.int32)[None, :]
    ).astype(jnp.int32)
    requests = jnp.sum(hits * local_ids[:, None], axis=0).reshape(wide_total, capacity)
    notes = lax.all_to_all(
        jnp.concatenate([requests, column_perm[0]], axis=1),
        "wide",
        split_axis=0,
        concat_axis=0,
        tiled=True,
    )
    asked, band_cols = notes[:, :capacity], notes[:, capacity:].reshape(slot_total)
    arrived = lax.all_to_all(projected[asked], "wide", split_axis=0, concat_axis=0, tiled=True)
    entry_blocks = arrived.reshape(entry_total, 8, BLOCK)[bucket_slot]
    slot_blocks = entry_blocks.reshape(slot_total, list_depth, 8, BLOCK)
    slot_lengths = list_lengths.reshape(slot_total)
    slot_rows = jnp.repeat(jnp.arange(row_total, dtype=jnp.int32), per_row)
    slot_cols = column_perm.reshape(slot_total)
    scalars = jnp.concatenate(
        [jnp.stack(conic_form), camera_matrix_row[:4], jnp.zeros((1,), jnp.float32)]
    )
    colors = draw_tiles(slot_lengths, slot_cols, slot_rows, scalars, slot_blocks)
    sending = colors.reshape(row_total, per_row, 3, TILE * TILE)
    band_tiles = lax.all_to_all(sending, "wide", split_axis=0, concat_axis=0, tiled=True)
    band_tiles = band_tiles.reshape(slot_total, 3, TILE * TILE)
    column_ids = jnp.arange(slot_total, dtype=jnp.int32)
    placement = jnp.sum(
        column_ids[:, None] * (band_cols[:, None] == column_ids[None, :]).astype(jnp.int32), axis=0
    )
    image_band = (
        band_tiles[placement]
        .reshape(slot_total, 3, TILE, TILE)
        .transpose(1, 2, 0, 3)
        .reshape(3, TILE, slot_total * TILE)
    )
    margin = HALF
    paired = jnp.stack([image_band, target[0]])
    extended = with_halo(paired, (("wide", 2),), margin)
    loss_scale = 3.0 * view_total
    row_weight = jnp.ones((TILE,), jnp.float32)
    grad_rows = jax.grad(
        lambda rows_now: structure_loss(rows_now, extended[1], TILE, row_weight, loss_scale)
    )(extended[0])
    band_grad = grad_rows[:, HALF : HALF + TILE]
    rim_rows = jnp.concatenate([grad_rows[:, :HALF], grad_rows[:, HALF + TILE :]], axis=1)
    received = with_halo(rim_rows, (("wide", 1),), HALF)
    band_grad = (
        band_grad.at[:, :HALF]
        .add(received[:, :HALF])
        .at[:, TILE - HALF :]
        .add(received[:, 3 * HALF :])
    )
    grad_tiles = (
        band_grad.reshape(3, TILE, slot_total, TILE)
        .transpose(2, 0, 1, 3)
        .reshape(slot_total, 3, TILE * TILE)
    )
    by_slot = grad_tiles[band_cols].reshape(
        wide_total, per_row, 3, TILE * TILE
    )
    color_grads = lax.all_to_all(by_slot, "wide", split_axis=0, concat_axis=0, tiled=True).reshape(
        slot_total, 3, TILE * TILE
    )
    once = jnp.pad(color_grads, ((0, 0), (0, 1), (0, 0)))
    high = lax.reduce_precision(once, 8, 7)
    doubled = jnp.concatenate([high, high, once - high, jnp.zeros_like(once)], axis=1).astype(
        jnp.bfloat16
    )
    entry_grads = pull_tiles(slot_lengths, slot_cols, slot_rows, scalars, slot_blocks, doubled)
    entry_grads = entry_grads.reshape(entry_total, 8 * BLOCK).astype(jnp.bfloat16)
    returning = jnp.dot(
        hits.T.astype(jnp.bfloat16), entry_grads, preferred_element_type=jnp.float32
    ).astype(jnp.bfloat16)
    returned = lax.all_to_all(
        returning.reshape(wide_total, capacity, 8 * BLOCK)[:, :, : 7 * BLOCK],
        "wide",
        split_axis=0,
        concat_axis=0,
        tiled=True,
    ).reshape(entry_total, 7 * BLOCK)
    held_ids = jnp.arange(block_grand_total, dtype=jnp.int32)
    held_hits = (held_ids[:, None] == asked.reshape(entry_total)[None, :]).astype(jnp.bfloat16)
    partial_rows = (
        jnp.dot(held_hits, returned, preferred_element_type=jnp.float32)
        .astype(jnp.bfloat16)
        .reshape(block_grand_total, 7, BLOCK)
    )
    splat_grads = add_views(
        partial_rows.transpose(1, 0, 2).reshape(7, block_grand_total * BLOCK)
    )
    return (image_band[None], splat_grads)


def solution(mesh):
    in_specs = (
        P(None, "wide"),
        P("view", None),
        P("view", None, "wide"),
        P("view", None, "wide", None),
        P("view", None, "wide"),
        P("view", None, "wide", None),
    )
    out_specs = (P("view", None, "wide", None), P(None, "wide"))
    return jax.shard_map(
        on_device, mesh=mesh, in_specs=in_specs, out_specs=out_specs, check_vma=False
    )
```

profile of v0, /device:TPU:0, one launch (start us, length us, event | category | flops | bytes accessed | tf_op | source)
XLA Modules:
  0.0 300.2 jit_solution(17494121648794746426)
XLA Ops:
  0.6 0.8 copy.67
  1.4 0.8 copy.66
  3.6 7.3 %all-to-all-start = ((s32[8,1,20]{2,1,0:T(1,128)}), s32[8,1,20]{2,1,0:T(1,128)S(1)}, u32[]{:S(2)}, u32[]{:S(2)}) async-start(s32[8,1,20]{2,1,0:T(1,128)} %bitcast.13), calls=%async_computation | async-start | bytes 8192 | tf_op jit(solution)/shard_map/all_to_all | solution.py:389
  10.9 1.5 fusion.194
  16.1 1.4 copy.92
  17.5 1.8 add_dynamic-update-slice_fusion.1
  19.4 1.9 add_dynamic-update-slice_fusion
  26.9 1.6 gather_fusion
  28.4 6.0 %all-to-all-start.1 = ((f32[8,16,8,128]{3,2,1,0:T(8,128)}), f32[8,16,8,128]{3,2,1,0:T(8,128)S(1)}, u32[]{:S(2)}, u32[]{:S(2)}) async-start(f32[8,16,8,128]{3,2,1,0:T(8,128)} %bitcast.15), calls=%async_computation.1 | async-start | bytes 1048576 | tf_op jit(solution)/shard_map/all_to_all | solution.py:397
  34.7 13.7 %all-to-all-done.1 = f32[8,16,8,128]{3,2,1,0:T(8,128)S(1)} async-done(((f32[8,16,8,128]{3,2,1,0:T(8,128)}), f32[8,16,8,128]{3,2,1,0:T(8,128)S(1)}, u32[]{:S(2)}, u32[]{:S(2)}) %all-to-all-start.1) | async-done | bytes 524320 | tf_op jit(solution)/shard_map/all_to_all | solution.py:397
  49.2 41.6 %shard_map.77 = f32[32,3,1024]{2,1,0:T(4,128)S(1)} custom-call(s32[32]{0:T(128)S(1)} %reshape.338.lengths, s32[32]{0:T(128)S(1)} %reshape.339.cols, s32[32]{0:T(128)S(1)} %reshape.340.rows, f32[8]{0:T(128)S(1)} %concatenate.20.scalar_ref, f32[32,4,8,128]{3,2,1,0:T(8,128)S(1)} %bitcast.85, bf16[256,256]{1,0:T(8,128)(2,1)S(1)} %get-tuple-element.88.before_mat), custom_call_target="tpu_custom_call" | custom-call | tf_op jit(solution)/shard_map/pallas_call | solution.py:264
  90.7 1.0 copy.71
  91.7 14.7 %all-to-all-start.2 = ((f32[8,4,3,1024]{3,1,2,0:T(4,128)}), f32[8,4,3,1024]{3,1,2,0:T(4,128)S(1)}, u32[]{:S(2)}, u32[]{:S(2)}) async-start(f32[8,4,3,1024]{3,1,2,0:T(4,128)} %copy.71), calls=%async_computation.2 | async-start | bytes 786432 | tf_op jit(solution)/shard_map/all_to_all | solution.py:408
  106.7 9.0 %all-to-all-done.2 = f32[8,4,3,1024]{3,1,2,0:T(4,128)S(1)} async-done(((f32[8,4,3,1024]{3,1,2,0:T(4,128)}), f32[8,4,3,1024]{3,1,2,0:T(4,128)S(1)}, u32[]{:S(2)}, u32[]{:S(2)}) %all-to-all-start.2) | async-done | bytes 393248 | tf_op jit(solution)/shard_map/all_to_all | solution.py:408
  115.9 0.9 gather_fusion.2
  117.6 2.1 copy.74
  119.7 2.2 broadcast_in_dim_reshape.2
  122.0 3.1 %collective-permute-start = (f32[2,3,5,1024]{3,2,1,0:T(8,128)S(1)}, f32[2,3,5,1024]{3,2,1,0:T(8,128)S(1)}, u32[]{:S(2)}, u32[]{:S(2)}) collective-permute-start(f32[2,3,5,1024]{3,2,1,0:T(8,128)S(1)} %get-tuple-element.49), channel_id=1, source_target_pairs={{0,1},{1,2},{2,3},{3,4},{4,5},{5,6},{6,7},{8,9},{9,10},{10,11},{11... | collective-permute-start | bytes 368648 | tf_op jit(solution)/shard_map/ppermute | solution.py:28
  125.1 1.5 collective-permute-start.1
  126.5 1.7 collective-permute-done
  128.2 4.4 %collective-permute-done.1 = f32[2,3,5,1024]{3,2,1,0:T(8,128)S(1)} collective-permute-done((f32[2,3,5,1024]{3,2,1,0:T(8,128)S(1)}, f32[2,3,5,1024]{3,2,1,0:T(8,128)S(1)}, u32[]{:S(2)}, u32[]{:S(2)}) %collective-permute-start.1) | collective-permute-done | bytes 122912 | tf_op jit(solution)/shard_map/ppermute | solution.py:29
  133.1 1.6 fusion.10
  134.7 1.6 fusion.30
  136.3 1.6 fusion.90
  137.9 1.6 fusion.70
  139.5 1.6 fusion.50
  141.1 2.5 broadcast_multiply_fusion.18
  147.6 0.9 pad_add_fusion
  148.6 0.9 pad_add_fusion.1
  149.5 0.9 pad_add_fusion.2
  150.4 2.8 fusion.100
  153.3 3.2 %collective-permute-start.2 = (f32[3,5,1024]{2,1,0:T(8,128)S(1)}, f32[3,5,1024]{2,1,0:T(8,128)S(1)}, u32[]{:S(2)}, u32[]{:S(2)}) collective-permute-start(f32[3,5,1024]{2,1,0:T(8,128)S(1)} %get-tuple-element.52), channel_id=1, source_target_pairs={{0,1},{1,2},{2,3},{3,4},{4,5},{5,6},{6,7},{8,9},{9,10},{10,11},{11... | collective-permute-start | bytes 184328 | tf_op jit(solution)/shard_map/ppermute | solution.py:28
  156.5 1.3 collective-permute-start.3
  157.8 0.8 collective-permute-done.2
  159.3 3.7 %collective-permute-done.3 = f32[3,5,1024]{2,1,0:T(8,128)S(1)} collective-permute-done((f32[3,5,1024]{2,1,0:T(8,128)S(1)}, f32[3,5,1024]{2,1,0:T(8,128)S(1)}, u32[]{:S(2)}, u32[]{:S(2)}) %collective-permute-start.3) | collective-permute-done | bytes 61472 | tf_op jit(solution)/shard_map/ppermute | solution.py:29
  163.8 2.1 copy.91
  165.9 2.1 reshape.351
  168.3 0.9 gather_fusion.3
  169.2 1.0 copy.77
  170.2 3.8 %all-to-all-start.3 = ((f32[8,4,3,1024]{3,1,2,0:T(4,128)}), f32[8,4,3,1024]{3,1,2,0:T(4,128)S(1)}, u32[]{:S(2)}, u32[]{:S(2)}) async-start(f32[8,4,3,1024]{3,1,2,0:T(4,128)} %copy.77), calls=%async_computation.3 | async-start | bytes 786432 | tf_op jit(solution)/shard_map/all_to_all | solution.py:445
  174.1 9.1 %all-to-all-done.3 = f32[8,4,3,1024]{3,1,2,0:T(4,128)S(1)} async-done(((f32[8,4,3,1024]{3,1,2,0:T(4,128)}), f32[8,4,3,1024]{3,1,2,0:T(4,128)S(1)}, u32[]{:S(2)}, u32[]{:S(2)}) %all-to-all-start.3) | async-done | bytes 393248 | tf_op jit(solution)/shard_map/all_to_all | solution.py:445
  184.2 65.4 %shard_map.78 = f32[32,4,8,128]{3,2,1,0:T(8,128)S(1)} custom-call(s32[32]{0:T(128)S(1)} %reshape.338.lengths, s32[32]{0:T(128)S(1)} %reshape.339.cols, s32[32]{0:T(128)S(1)} %reshape.340.rows, f32[8]{0:T(128)S(1)} %concatenate.20.scalar_ref, f32[32,4,8,128]{3,2,1,0:T(8,128)S(1)} %bitcast.86, bf16[32,16,1024]{2,1,0:T(8,128)(2,1)S(1)} %maximum_maximum_fusion.grads, ...), custom_call_target="tpu_custom_call" | custom-call | tf_op jit(solution)/shard_map/pallas_call | solution.py:285
  250.6 21.6 %all-to-all-start.4 = ((bf16[8,16,896]{2,1,0:T(8,128)(2,1)}), bf16[8,16,896]{2,1,0:T(8,128)(2,1)S(1)}, u32[]{:S(2)}, u32[]{:S(2)}) async-start(bf16[8,16,896]{2,1,0:T(8,128)(2,1)} %slice.677), calls=%async_computation.4 | async-start | bytes 458752 | tf_op jit(solution)/shard_map/all_to_all | solution.py:458
  272.3 7.9 %all-to-all-done.4 = bf16[8,16,896]{2,1,0:T(8,128)(2,1)S(1)} async-done(((bf16[8,16,896]{2,1,0:T(8,128)(2,1)}), bf16[8,16,896]{2,1,0:T(8,128)(2,1)S(1)}, u32[]{:S(2)}, u32[]{:S(2)}) %all-to-all-start.4) | async-done | bytes 229408 | tf_op jit(solution)/shard_map/all_to_all | solution.py:458
  281.4 1.5 collective-permute-done.4
  283.1 14.0 %collective-permute-done.5 = f32[7,16384]{1,0:T(8,128)S(1)} collective-permute-done((f32[7,16384]{1,0:T(8,128)S(1)}, f32[7,16384]{1,0:T(8,128)S(1)}, u32[]{:S(2)}, u32[]{:S(2)}) %collective-permute-start.5) | collective-permute-done | bytes 458784 | tf_op jit(solution)/shard_map/ppermute | solution.py:351
  297.2 1.9 collective-permute-done.6
  299.2 1.1 pad_maximum_fusion.1
  (96 shorter events, 15.0 us)
Async XLA Ops:
  3.6 23.0 %all-to-all-start = ((s32[8,1,20]{2,1,0:T(1,128)}), s32[8,1,20]{2,1,0:T(1,128)S(1)}, u32[]{:S(2)}, u32[]{:S(2)}) async-start(s32[8,1,20]{2,1,0:T(1,128)} %bitcast.13), calls=%async_computation | async-start | bytes 8192 | tf_op jit(solution)/shard_map/all_to_all | solution.py:389
  17.5 7.9 %copy-start.3 = (s32[1,8,4]{1,2,0:T(4,128)S(1)}, s32[1,8,4]{1,2,0:T(4,128)}, u32[]{:S(2)}) copy-start(s32[1,8,4]{1,2,0:T(4,128)} %param.12) | copy-start | bytes 388
  17.5 8.1 %copy-start.4 = (s32[1,8,4]{1,2,0:T(4,128)S(1)}, s32[1,8,4]{1,2,0:T(4,128)}, u32[]{:S(2)}) copy-start(s32[1,8,4]{1,2,0:T(4,128)} %param.14) | copy-start | bytes 388
  26.6 7.8 %copy-start.2 = (f32[1,6]{1,0:T(1,128)S(1)}, f32[1,6]{1,0:T(1,128)}, u32[]{:S(2)}) copy-start(f32[1,6]{1,0:T(1,128)} %param.11) | copy-start | bytes 76
  28.4 20.0 %all-to-all-start.1 = ((f32[8,16,8,128]{3,2,1,0:T(8,128)}), f32[8,16,8,128]{3,2,1,0:T(8,128)S(1)}, u32[]{:S(2)}, u32[]{:S(2)}) async-start(f32[8,16,8,128]{3,2,1,0:T(8,128)} %bitcast.15), calls=%async_computation.1 | async-start | bytes 1048576 | tf_op jit(solution)/shard_map/all_to_all | solution.py:397
  91.7 23.9 %all-to-all-start.2 = ((f32[8,4,3,1024]{3,1,2,0:T(4,128)}), f32[8,4,3,1024]{3,1,2,0:T(4,128)S(1)}, u32[]{:S(2)}, u32[]{:S(2)}) async-start(f32[8,4,3,1024]{3,1,2,0:T(4,128)} %copy.71), calls=%async_computation.2 | async-start | bytes 786432 | tf_op jit(solution)/shard_map/all_to_all | solution.py:408
  119.7 2.2 copy-start.1
  121.9 11.0 %copy-start = (f32[1,3,32,1024]{3,2,1,0:T(8,128)}, f32[1,3,32,1024]{3,2,1,0:T(8,128)S(1)}, u32[]{:S(2)}) copy-start(f32[1,3,32,1024]{3,2,1,0:T(8,128)S(1)} %broadcast_in_dim_reshape.2) | copy-start | bytes 1179652
  122.0 6.2 %collective-permute-start = (f32[2,3,5,1024]{3,2,1,0:T(8,128)S(1)}, f32[2,3,5,1024]{3,2,1,0:T(8,128)S(1)}, u32[]{:S(2)}, u32[]{:S(2)}) collective-permute-start(f32[2,3,5,1024]{3,2,1,0:T(8,128)S(1)} %get-tuple-element.49), channel_id=1, source_target_pairs={{0,1},{1,2},{2,3},{3,4},{4,5},{5,6},{6,7},{8,9},{9,10},{10,11},{11... | collective-permute-start | bytes 368648 | tf_op jit(solution)/shard_map/ppermute | solution.py:28
  125.1 7.6 %collective-permute-start.1 = (f32[2,3,5,1024]{3,2,1,0:T(8,128)S(1)}, f32[2,3,5,1024]{3,2,1,0:T(8,128)S(1)}, u32[]{:S(2)}, u32[]{:S(2)}) collective-permute-start(f32[2,3,5,1024]{3,2,1,0:T(8,128)S(1)} %get-tuple-element.50), channel_id=1, source_target_pairs={{1,0},{2,1},{3,2},{4,3},{5,4},{6,5},{7,6},{9,8},{10,9},{11,10},{12... | collective-permute-start | bytes 368648 | tf_op jit(solution)/shard_map/ppermute | solution.py:29
  153.3 5.4 %collective-permute-start.2 = (f32[3,5,1024]{2,1,0:T(8,128)S(1)}, f32[3,5,1024]{2,1,0:T(8,128)S(1)}, u32[]{:S(2)}, u32[]{:S(2)}) collective-permute-start(f32[3,5,1024]{2,1,0:T(8,128)S(1)} %get-tuple-element.52), channel_id=1, source_target_pairs={{0,1},{1,2},{2,3},{3,4},{4,5},{5,6},{6,7},{8,9},{9,10},{10,11},{11... | collective-permute-start | bytes 184328 | tf_op jit(solution)/shard_map/ppermute | solution.py:28
  156.5 6.5 %collective-permute-start.3 = (f32[3,5,1024]{2,1,0:T(8,128)S(1)}, f32[3,5,1024]{2,1,0:T(8,128)S(1)}, u32[]{:S(2)}, u32[]{:S(2)}) collective-permute-start(f32[3,5,1024]{2,1,0:T(8,128)S(1)} %get-tuple-element.51), channel_id=1, source_target_pairs={{1,0},{2,1},{3,2},{4,3},{5,4},{6,5},{7,6},{9,8},{10,9},{11,10},{12... | collective-permute-start | bytes 184328 | tf_op jit(solution)/shard_map/ppermute | solution.py:29
  170.2 13.0 %all-to-all-start.3 = ((f32[8,4,3,1024]{3,1,2,0:T(4,128)}), f32[8,4,3,1024]{3,1,2,0:T(4,128)S(1)}, u32[]{:S(2)}, u32[]{:S(2)}) async-start(f32[8,4,3,1024]{3,1,2,0:T(4,128)} %copy.77), calls=%async_computation.3 | async-start | bytes 786432 | tf_op jit(solution)/shard_map/all_to_all | solution.py:445
  250.6 29.6 %all-to-all-start.4 = ((bf16[8,16,896]{2,1,0:T(8,128)(2,1)}), bf16[8,16,896]{2,1,0:T(8,128)(2,1)S(1)}, u32[]{:S(2)}, u32[]{:S(2)}) async-start(bf16[8,16,896]{2,1,0:T(8,128)(2,1)} %slice.677), calls=%async_computation.4 | async-start | bytes 458752 | tf_op jit(solution)/shard_map/all_to_all | solution.py:458
  281.3 1.6 collective-permute-start.4
  283.0 14.0 %collective-permute-start.5 = (f32[7,16384]{1,0:T(8,128)S(1)}, f32[7,16384]{1,0:T(8,128)S(1)}, u32[]{:S(2)}, u32[]{:S(2)}) collective-permute-start(f32[7,16384]{1,0:T(8,128)S(1)} %convert_add_fusion), channel_id=1, source_target_pairs={{0,16},{8,24},{16,0},{24,8},{1,17},{9,25},{17,1},{25,9},{2,18},{10... | collective-permute-start | bytes 1376264 | tf_op jit(solution)/shard_map/ppermute | solution.py:351
  297.1 2.0 collective-permute-start.6
where the time goes:
time: 303 us; the launch traced here: 300 us
  Pallas kernels  107 us (35%)
  waiting for transfers between devices  67.8 us (22%)
  starting transfers between devices  62.7 us (21%)
  other arithmetic  27.9 us (9%)
  local copies, waits for them, and re-layouts  25.6 us (8%)
  between operations  8.88 us (3%)
    pallas_call x1, Pallas kernels, pull_tiles(): pl.pallas_call(pull_kernel, grid_spec=pltpu.PrefetchScalarGridSpec(num_sc...  65.4 us
    pallas_call x1, Pallas kernels, draw_tiles(): pl.pallas_call(functools.partial(draw_kernel, group), grid_spec=pltpu.Pre...  41.6 us
    all_to_all x1, starting transfers between devices, on_device(): lax.all_to_all(returning.reshape(wide_total, capacity, 8 * BLOCK)[:, :, :...  21.6 us
    all_to_all x1, starting transfers between devices, on_device(): lax.all_to_all(sending, 'wide', split_axis=0, concat_axis=0, tiled=True)  14.7 us
    ppermute x1, waiting for transfers between devices, add_views(): lax.ppermute(pair_sum, 'view', [(i, (i + 2 * step) % views) for i in rang...  14 us
    all_to_all x1, waiting for transfers between devices, on_device(): lax.all_to_all(projected[asked], 'wide', split_axis=0, concat_axis=0, til...  13.7 us
    all_to_all x1, waiting for transfers between devices, on_device(): lax.all_to_all(by_slot, 'wide', split_axis=0, concat_axis=0, tiled=True)  9.12 us
    all_to_all x1, waiting for transfers between devices, on_device(): lax.all_to_all(sending, 'wide', split_axis=0, concat_axis=0, tiled=True)  9.01 us
  transfers between devices with their start and end apart: 12, of which 11 were waited for; matrix products, arithmetic and copies ran while one was open for 3% of the time, Pallas kernels for 0%

commit v1 on v0

--- a/solution.py
+++ b/solution.py
@@ -67,7 +67,7 @@
     return (second / determinant, -mixed / determinant, first / determinant)
 
 
-CHUNK = 8
+CHUNK = 16
 PIXELS = TILE * TILE
 SPAN = CHUNK * TILE
 LOG2E = math.log2(math.e)
@@ -339,25 +339,14 @@
     return jnp.sum(row_weight[None, :, None] * (1.0 - numerator / denominator)) / loss_scale
 
 
-def add_views(partial):
+def from_views(values):
     views = lax.axis_size("view")
-    half = partial.shape[1] // 2
-    odd = lax.rem(lax.axis_index("view"), 2) == 1
     mates = [(i, i ^ 1) for i in range(views)]
-    left, right = partial[:, :half], partial[:, half:]
-    theirs = lax.ppermute(jnp.where(odd, left, right), "view", mates)
-    pair_sum = jnp.where(odd, right, left).astype(jnp.float32) + theirs.astype(jnp.float32)
-    others = [
-        lax.ppermute(pair_sum, "view", [(i, (i + 2 * step) % views) for i in range(views)])
+    own_side = [values] + [
+        lax.ppermute(values, "view", [(i, (i + 2 * step) % views) for i in range(views)])
         for step in range(1, views // 2)
     ]
-    total = pair_sum
-    for other in others:
-        total = total + other
-    mate_total = lax.ppermute(total, "view", mates)
-    return jnp.concatenate(
-        [jnp.where(odd, mate_total, total), jnp.where(odd, total, mate_total)], axis=1
-    )
+    return own_side + [lax.ppermute(each, "view", mates) for each in own_side]
 
 
 def on_device(splats, camera, column_perm, block_lists, list_lengths, target):
@@ -394,6 +383,7 @@
         tiled=True,
     )
     asked, band_cols = notes[:, :capacity], notes[:, capacity:].reshape(slot_total)
+    view_ids = from_views(asked.reshape(entry_total))
     arrived = lax.all_to_all(projected[asked], "wide", split_axis=0, concat_axis=0, tiled=True)
     entry_blocks = arrived.reshape(entry_total, 8, BLOCK)[bucket_slot]
     slot_blocks = entry_blocks.reshape(slot_total, list_depth, 8, BLOCK)
@@ -463,14 +453,14 @@
         tiled=True,
     ).reshape(entry_total, 7 * BLOCK)
     held_ids = jnp.arange(block_grand_total, dtype=jnp.int32)
-    held_hits = (held_ids[:, None] == asked.reshape(entry_total)[None, :]).astype(jnp.bfloat16)
-    partial_rows = (
-        jnp.dot(held_hits, returned, preferred_element_type=jnp.float32)
-        .astype(jnp.bfloat16)
+    all_ids = jnp.concatenate(view_ids, axis=0)
+    held_hits = (held_ids[:, None] == all_ids[None, :]).astype(jnp.bfloat16)
+    all_rows = jnp.concatenate(from_views(returned), axis=0)
+    splat_grads = (
+        jnp.dot(held_hits, all_rows, preferred_element_type=jnp.float32)
         .reshape(block_grand_total, 7, BLOCK)
-    )
-    splat_grads = add_views(
-        partial_rows.transpose(1, 0, 2).reshape(7, block_grand_total * BLOCK)
+        .transpose(1, 0, 2)
+        .reshape(7, block_grand_total * BLOCK)
     )
     return (image_band[None], splat_grads)
 

time: 303 us -> 277 us (0.914)
  starting transfers between devices: 62.7 us -> 36.7 us
  blocking collectives: 0 us -> 15.9 us
  waiting for transfers between devices: 67.8 us -> 54 us
    all_to_all x1 -> x0, starting transfers between devices: 21.6 us -> none  [on_device(): lax.all_to_all(returning.reshape(wide_total, capacity, 8 * BLOCK)[:, :, :...]
    all_to_all x0 -> x1, blocking collectives: none -> 15.9 us  [on_device(): lax.all_to_all(returning.reshape(wide_total, capacity, 8 * BLOCK)[:, :, :...]
    all_to_all x1, starting transfers between devices: 14.7 us -> 5.4 us  [on_device(): lax.all_to_all(sending, 'wide', split_axis=0, concat_axis=0, tiled=True)]
    ppermute x3 -> x6, waiting for transfers between devices: 17.4 us -> 8.74 us  [the longest x2 7.62 us: from_views(): lax.ppermute(values, 'view', [(i, (i + 2 * step) % views) for i in range(...]
    all_to_all x1 -> x0, waiting for transfers between devices: 7.92 us -> none  [on_device(): lax.all_to_all(returning.reshape(wide_total, capacity, 8 * BLOCK)[:, :, :...]
    ppermute x3 -> x6, starting transfers between devices: 0.21 us -> 3.33 us  [the longest x2 3.02 us: from_views(): lax.ppermute(values, 'view', [(i, (i + 2 * step) % views) for i in range(...]
  transfers between devices with their start and end apart: 12 -> 14, of which waited for: 11 -> 10; matrix products, arithmetic and copies ran while one was open for 3% -> 3% of each run, Pallas kernels for 0% -> 0%
where the time goes in v1:
time: 277 us; the launch traced here: 275 us
  Pallas kernels  106 us (38%)
  waiting for transfers between devices  54 us (19%)
  starting transfers between devices  36.7 us (13%)
  other arithmetic  26.5 us (10%)
  local copies, waits for them, and re-layouts  25.9 us (9%)
  blocking collectives  15.9 us (6%)
  between operations  8.85 us (3%)
    pallas_call x1, Pallas kernels, pull_tiles(): pl.pallas_call(pull_kernel, grid_spec=pltpu.PrefetchScalarGridSpec(num_sc...  66.6 us
    pallas_call x1, Pallas kernels, draw_tiles(): pl.pallas_call(functools.partial(draw_kernel, group), grid_spec=pltpu.Pre...  39.8 us
    all_to_all x1, blocking collectives, on_device(): lax.all_to_all(returning.reshape(wide_total, capacity, 8 * BLOCK)[:, :, :...  15.9 us
    all_to_all x1, waiting for transfers between devices, on_device(): lax.all_to_all(projected[asked], 'wide', split_axis=0, concat_axis=0, til...  13.7 us
    all_to_all x1, waiting for transfers between devices, on_device(): lax.all_to_all(sending, 'wide', split_axis=0, concat_axis=0, tiled=True)  11.1 us
    all_to_all x1, waiting for transfers between devices, on_device(): lax.all_to_all(by_slot, 'wide', split_axis=0, concat_axis=0, tiled=True)  9.83 us
    add x5, other arithmetic, blur_field(): across + tap_list[offset] * padded_input[:, :, offset:offset + field_width]  7.92 us
    ppermute x2, waiting for transfers between devices, from_views(): lax.ppermute(values, 'view', [(i, (i + 2 * step) % views) for i in range(...  7.62 us
  transfers between devices with their start and end apart: 14, of which 10 were waited for; matrix products, arithmetic and copies ran while one was open for 3% of the time, Pallas kernels for 0%

profile of v1, /device:TPU:0, one launch (start us, length us, event | category | flops | bytes accessed | tf_op | source)
XLA Modules:
  0.0 275.1 jit_solution(9022196516672211302)
XLA Ops:
  1.4 0.8 copy.66
  3.6 7.3 %all-to-all-start = ((s32[8,1,20]{2,1,0:T(1,128)}), s32[8,1,20]{2,1,0:T(1,128)S(1)}, u32[]{:S(2)}, u32[]{:S(2)}) async-start(s32[8,1,20]{2,1,0:T(1,128)} %bitcast.13), calls=%async_computation | async-start | bytes 8192 | tf_op jit(solution)/shard_map/all_to_all | solution.py:378
  10.9 1.5 fusion.203
  16.1 1.4 copy.94
  17.5 1.8 add_dynamic-update-slice_fusion.1
  19.4 1.9 add_dynamic-update-slice_fusion
  26.9 1.6 gather_fusion
  28.4 6.0 %all-to-all-start.1 = ((f32[8,16,8,128]{3,2,1,0:T(8,128)}), f32[8,16,8,128]{3,2,1,0:T(8,128)S(1)}, u32[]{:S(2)}, u32[]{:S(2)}) async-start(f32[8,16,8,128]{3,2,1,0:T(8,128)} %bitcast.15), calls=%async_computation.1 | async-start | bytes 1048576 | tf_op jit(solution)/shard_map/all_to_all | solution.py:387
  34.7 13.7 %all-to-all-done.1 = f32[8,16,8,128]{3,2,1,0:T(8,128)S(1)} async-done(((f32[8,16,8,128]{3,2,1,0:T(8,128)}), f32[8,16,8,128]{3,2,1,0:T(8,128)S(1)}, u32[]{:S(2)}, u32[]{:S(2)}) %all-to-all-start.1) | async-done | bytes 524320 | tf_op jit(solution)/shard_map/all_to_all | solution.py:387
  49.2 39.8 %shard_map.77 = f32[32,3,1024]{2,1,0:T(4,128)S(1)} custom-call(s32[32]{0:T(128)S(1)} %reshape.341.lengths, s32[32]{0:T(128)S(1)} %reshape.342.cols, s32[32]{0:T(128)S(1)} %reshape.343.rows, f32[8]{0:T(128)S(1)} %concatenate.23.scalar_ref, f32[32,4,8,128]{3,2,1,0:T(8,128)S(1)} %bitcast.84, bf16[256,256]{1,0:T(8,128)(2,1)S(1)} %get-tuple-element.86.before_mat), custom_call_target="tpu_custom_call" | custom-call | tf_op jit(solution)/shard_map/pallas_call | solution.py:264
  89.0 1.0 copy.71
  90.0 5.4 %all-to-all-start.2 = ((f32[8,4,3,1024]{3,1,2,0:T(4,128)}), f32[8,4,3,1024]{3,1,2,0:T(4,128)S(1)}, u32[]{:S(2)}, u32[]{:S(2)}) async-start(f32[8,4,3,1024]{3,1,2,0:T(4,128)} %copy.71), calls=%async_computation.2 | async-start | bytes 786432 | tf_op jit(solution)/shard_map/all_to_all | solution.py:398
  95.6 11.1 %all-to-all-done.2 = f32[8,4,3,1024]{3,1,2,0:T(4,128)S(1)} async-done(((f32[8,4,3,1024]{3,1,2,0:T(4,128)}), f32[8,4,3,1024]{3,1,2,0:T(4,128)S(1)}, u32[]{:S(2)}, u32[]{:S(2)}) %all-to-all-start.2) | async-done | bytes 393248 | tf_op jit(solution)/shard_map/all_to_all | solution.py:398
  107.0 0.9 gather_fusion.2
  108.6 2.1 copy.74
  110.7 2.2 broadcast_in_dim_reshape.4
  113.0 3.3 %collective-permute-start.3 = (f32[2,3,5,1024]{3,2,1,0:T(8,128)S(1)}, f32[2,3,5,1024]{3,2,1,0:T(8,128)S(1)}, u32[]{:S(2)}, u32[]{:S(2)}) collective-permute-start(f32[2,3,5,1024]{3,2,1,0:T(8,128)S(1)} %get-tuple-element.47), channel_id=1, source_target_pairs={{0,1},{1,2},{2,3},{3,4},{4,5},{5,6},{6,7},{8,9},{9,10},{10,11},{11... | collective-permute-start | bytes 368648 | tf_op jit(solution)/shard_map/ppermute | solution.py:28
  116.4 1.5 collective-permute-start.4
  117.9 3.1 %collective-permute-done.3 = f32[2,3,5,1024]{3,2,1,0:T(8,128)S(1)} collective-permute-done((f32[2,3,5,1024]{3,2,1,0:T(8,128)S(1)}, f32[2,3,5,1024]{3,2,1,0:T(8,128)S(1)}, u32[]{:S(2)}, u32[]{:S(2)}) %collective-permute-start.3) | collective-permute-done | bytes 122912 | tf_op jit(solution)/shard_map/ppermute | solution.py:28
  121.0 3.0 %collective-permute-done.4 = f32[2,3,5,1024]{3,2,1,0:T(8,128)S(1)} collective-permute-done((f32[2,3,5,1024]{3,2,1,0:T(8,128)S(1)}, f32[2,3,5,1024]{3,2,1,0:T(8,128)S(1)}, u32[]{:S(2)}, u32[]{:S(2)}) %collective-permute-start.4) | collective-permute-done | bytes 122912 | tf_op jit(solution)/shard_map/ppermute | solution.py:29
  124.4 1.6 fusion.18
  126.0 1.6 fusion.38
  127.6 1.6 fusion.98
  129.2 1.6 fusion.78
  130.8 1.6 fusion.58
  132.4 2.5 broadcast_multiply_fusion.18
  138.9 0.9 pad_add_fusion
  139.9 0.9 pad_add_fusion.1
  140.8 0.9 pad_add_fusion.2
  141.7 2.8 %fusion.108 = f32[3,42,1024]{2,1,0:T(8,128)S(1)} fusion(f32[3,42,1024]{2,1,0:T(8,128)S(1)} %get-tuple-element.65, f32[3,42,1024]{2,1,0:T(8,128)S(1)} %get-tuple-element.64, f32[3,42,1024]{2,1,0:T(8,128)S(1)} %get-tuple-element.63, f32[3,42,1024]{2,1,0:T(8,128)S(1)} %get-tuple-element.62, f32[3,42,1024]{2,1,0:T(8,128)S(1)} %get-tuple-element.61, ...), kind=kLoop, calls=%fused_computation.175 | loop fusion | flops 2967552 | bytes 12386304 | tf_op jit(solution)/shard_map/transpose(jvp())/add_any | solution.py:319
  144.6 3.7 %collective-permute-start.5 = (f32[3,5,1024]{2,1,0:T(8,128)S(1)}, f32[3,5,1024]{2,1,0:T(8,128)S(1)}, u32[]{:S(2)}, u32[]{:S(2)}) collective-permute-start(f32[3,5,1024]{2,1,0:T(8,128)S(1)} %get-tuple-element.50), channel_id=1, source_target_pairs={{0,1},{1,2},{2,3},{3,4},{4,5},{5,6},{6,7},{8,9},{9,10},{10,11},{11... | collective-permute-start | bytes 184328 | tf_op jit(solution)/shard_map/ppermute | solution.py:28
  148.4 1.3 collective-permute-start.6
  149.7 0.8 collective-permute-done.5
  151.1 3.7 %collective-permute-done.6 = f32[3,5,1024]{2,1,0:T(8,128)S(1)} collective-permute-done((f32[3,5,1024]{2,1,0:T(8,128)S(1)}, f32[3,5,1024]{2,1,0:T(8,128)S(1)}, u32[]{:S(2)}, u32[]{:S(2)}) %collective-permute-start.6) | collective-permute-done | bytes 61472 | tf_op jit(solution)/shard_map/ppermute | solution.py:29
  155.7 2.1 copy.92
  157.8 2.1 reshape.355
  160.2 0.9 gather_fusion.3
  161.0 1.0 copy.77
  162.0 4.8 %all-to-all-start.3 = ((f32[8,4,3,1024]{3,1,2,0:T(4,128)}), f32[8,4,3,1024]{3,1,2,0:T(4,128)S(1)}, u32[]{:S(2)}, u32[]{:S(2)}) async-start(f32[8,4,3,1024]{3,1,2,0:T(4,128)} %copy.77), calls=%async_computation.3 | async-start | bytes 786432 | tf_op jit(solution)/shard_map/all_to_all | solution.py:435
  167.0 9.8 %all-to-all-done.3 = f32[8,4,3,1024]{3,1,2,0:T(4,128)S(1)} async-done(((f32[8,4,3,1024]{3,1,2,0:T(4,128)}), f32[8,4,3,1024]{3,1,2,0:T(4,128)S(1)}, u32[]{:S(2)}, u32[]{:S(2)}) %all-to-all-start.3) | async-done | bytes 393248 | tf_op jit(solution)/shard_map/all_to_all | solution.py:435
  177.8 66.6 %shard_map.78 = f32[32,4,8,128]{3,2,1,0:T(8,128)S(1)} custom-call(s32[32]{0:T(128)S(1)} %reshape.341.lengths, s32[32]{0:T(128)S(1)} %reshape.342.cols, s32[32]{0:T(128)S(1)} %reshape.343.rows, f32[8]{0:T(128)S(1)} %concatenate.23.scalar_ref, f32[32,4,8,128]{3,2,1,0:T(8,128)S(1)} %bitcast.85, bf16[32,16,1024]{2,1,0:T(8,128)(2,1)S(1)} %maximum_maximum_fusion.grads, ...), custom_call_target="tpu_custom_call" | custom-call | tf_op jit(solution)/shard_map/pallas_call | solution.py:285
  244.7 15.9 %all_to_all.32 = bf16[8,16,896]{2,1,0:T(8,128)(2,1)S(1)} all-to-all(bf16[8,16,896]{2,1,0:T(8,128)(2,1)S(1)} %slice.669), channel_id=1, replica_groups=mesh['view'=4,'wide'=8] {'wide'}, dimensions={0} | all-to-all | bytes 458752 | tf_op jit(solution)/shard_map/all_to_all | solution.py:448
  260.6 1.3 collective-permute-start.7
  262.0 6.0 %collective-permute-done.7 = bf16[128,896]{1,0:T(8,128)(2,1)S(1)} collective-permute-done((bf16[128,896]{1,0:T(8,128)(2,1)S(1)}, bf16[128,896]{1,0:T(8,128)(2,1)S(1)}, u32[]{:S(2)}, u32[]{:S(2)}) %collective-permute-start.7) | collective-permute-done | bytes 229408 | tf_op jit(solution)/shard_map/ppermute | solution.py:346
  268.1 1.7 collective-permute-start
  270.1 1.6 collective-permute-done
  271.6 1.1 collective-permute-done.2
  273.6 1.5 copy.93
  (96 shorter events, 14.7 us)
Async XLA Ops:
  3.6 23.0 %all-to-all-start = ((s32[8,1,20]{2,1,0:T(1,128)}), s32[8,1,20]{2,1,0:T(1,128)S(1)}, u32[]{:S(2)}, u32[]{:S(2)}) async-start(s32[8,1,20]{2,1,0:T(1,128)} %bitcast.13), calls=%async_computation | async-start | bytes 8192 | tf_op jit(solution)/shard_map/all_to_all | solution.py:378
  17.5 7.9 %copy-start.3 = (s32[1,8,4]{1,2,0:T(4,128)S(1)}, s32[1,8,4]{1,2,0:T(4,128)}, u32[]{:S(2)}) copy-start(s32[1,8,4]{1,2,0:T(4,128)} %param.12) | copy-start | bytes 388
  17.5 8.1 %copy-start.4 = (s32[1,8,4]{1,2,0:T(4,128)S(1)}, s32[1,8,4]{1,2,0:T(4,128)}, u32[]{:S(2)}) copy-start(s32[1,8,4]{1,2,0:T(4,128)} %param.14) | copy-start | bytes 388
  26.6 7.8 %copy-start.2 = (f32[1,6]{1,0:T(1,128)S(1)}, f32[1,6]{1,0:T(1,128)}, u32[]{:S(2)}) copy-start(f32[1,6]{1,0:T(1,128)} %param.11) | copy-start | bytes 76
  28.4 20.0 %all-to-all-start.1 = ((f32[8,16,8,128]{3,2,1,0:T(8,128)}), f32[8,16,8,128]{3,2,1,0:T(8,128)S(1)}, u32[]{:S(2)}, u32[]{:S(2)}) async-start(f32[8,16,8,128]{3,2,1,0:T(8,128)} %bitcast.15), calls=%async_computation.1 | async-start | bytes 1048576 | tf_op jit(solution)/shard_map/all_to_all | solution.py:387
  90.0 16.7 %all-to-all-start.2 = ((f32[8,4,3,1024]{3,1,2,0:T(4,128)}), f32[8,4,3,1024]{3,1,2,0:T(4,128)S(1)}, u32[]{:S(2)}, u32[]{:S(2)}) async-start(f32[8,4,3,1024]{3,1,2,0:T(4,128)} %copy.71), calls=%async_computation.2 | async-start | bytes 786432 | tf_op jit(solution)/shard_map/all_to_all | solution.py:398
  110.7 2.2 copy-start.1
  112.9 11.2 %copy-start = (f32[1,3,32,1024]{3,2,1,0:T(8,128)}, f32[1,3,32,1024]{3,2,1,0:T(8,128)S(1)}, u32[]{:S(2)}) copy-start(f32[1,3,32,1024]{3,2,1,0:T(8,128)S(1)} %broadcast_in_dim_reshape.4) | copy-start | bytes 1179652
  113.0 7.9 %collective-permute-start.3 = (f32[2,3,5,1024]{3,2,1,0:T(8,128)S(1)}, f32[2,3,5,1024]{3,2,1,0:T(8,128)S(1)}, u32[]{:S(2)}, u32[]{:S(2)}) collective-permute-start(f32[2,3,5,1024]{3,2,1,0:T(8,128)S(1)} %get-tuple-element.47), channel_id=1, source_target_pairs={{0,1},{1,2},{2,3},{3,4},{4,5},{5,6},{6,7},{8,9},{9,10},{10,11},{11... | collective-permute-start | bytes 368648 | tf_op jit(solution)/shard_map/ppermute | solution.py:28
  116.4 7.6 %collective-permute-start.4 = (f32[2,3,5,1024]{3,2,1,0:T(8,128)S(1)}, f32[2,3,5,1024]{3,2,1,0:T(8,128)S(1)}, u32[]{:S(2)}, u32[]{:S(2)}) collective-permute-start(f32[2,3,5,1024]{3,2,1,0:T(8,128)S(1)} %get-tuple-element.48), channel_id=1, source_target_pairs={{1,0},{2,1},{3,2},{4,3},{5,4},{6,5},{7,6},{9,8},{10,9},{11,10},{12... | collective-permute-start | bytes 368648 | tf_op jit(solution)/shard_map/ppermute | solution.py:29
  144.6 5.9 %collective-permute-start.5 = (f32[3,5,1024]{2,1,0:T(8,128)S(1)}, f32[3,5,1024]{2,1,0:T(8,128)S(1)}, u32[]{:S(2)}, u32[]{:S(2)}) collective-permute-start(f32[3,5,1024]{2,1,0:T(8,128)S(1)} %get-tuple-element.50), channel_id=1, source_target_pairs={{0,1},{1,2},{2,3},{3,4},{4,5},{5,6},{6,7},{8,9},{9,10},{10,11},{11... | collective-permute-start | bytes 184328 | tf_op jit(solution)/shard_map/ppermute | solution.py:28
  148.4 6.5 %collective-permute-start.6 = (f32[3,5,1024]{2,1,0:T(8,128)S(1)}, f32[3,5,1024]{2,1,0:T(8,128)S(1)}, u32[]{:S(2)}, u32[]{:S(2)}) collective-permute-start(f32[3,5,1024]{2,1,0:T(8,128)S(1)} %get-tuple-element.49), channel_id=1, source_target_pairs={{1,0},{2,1},{3,2},{4,3},{5,4},{6,5},{7,6},{9,8},{10,9},{11,10},{12... | collective-permute-start | bytes 184328 | tf_op jit(solution)/shard_map/ppermute | solution.py:29
  162.0 14.7 %all-to-all-start.3 = ((f32[8,4,3,1024]{3,1,2,0:T(4,128)}), f32[8,4,3,1024]{3,1,2,0:T(4,128)S(1)}, u32[]{:S(2)}, u32[]{:S(2)}) async-start(f32[8,4,3,1024]{3,1,2,0:T(4,128)} %copy.77), calls=%async_computation.3 | async-start | bytes 786432 | tf_op jit(solution)/shard_map/all_to_all | solution.py:435
  260.6 7.4 %collective-permute-start.7 = (bf16[128,896]{1,0:T(8,128)(2,1)S(1)}, bf16[128,896]{1,0:T(8,128)(2,1)S(1)}, u32[]{:S(2)}, u32[]{:S(2)}) collective-permute-start(bf16[128,896]{1,0:T(8,128)(2,1)S(1)} %bitcast.104), channel_id=1, source_target_pairs={{0,16},{8,24},{16,0},{24,8},{1,17},{9,25},{17,1},{25,9},{2,18},{10... | collective-permute-start | bytes 688136 | tf_op jit(solution)/shard_map/ppermute | solution.py:346
  261.9 10.9 %collective-permute-start.8 = (bf16[128,896]{1,0:T(8,128)(2,1)S(1)}, bf16[128,896]{1,0:T(8,128)(2,1)S(1)}, u32[]{:S(2)}, u32[]{:S(2)}) collective-permute-start(bf16[128,896]{1,0:T(8,128)(2,1)S(1)} %bitcast.105), channel_id=1, source_target_pairs={{0,8},{8,0},{16,24},{24,16},{1,9},{9,1},{17,25},{25,17},{2,10},{10... | collective-permute-start | bytes 688136 | tf_op jit(solution)/shard_map/ppermute | solution.py:349
  268.0 4.8 %collective-permute-start.9 = (bf16[128,896]{1,0:T(8,128)(2,1)S(1)}, bf16[128,896]{1,0:T(8,128)(2,1)S(1)}, u32[]{:S(2)}, u32[]{:S(2)}) collective-permute-start(bf16[128,896]{1,0:T(8,128)(2,1)S(1)} %collective-permute-done.7), channel_id=1, source_target_pairs={{0,8},{8,0},{16,24},{24,16},{1,9},{9,1},{17,25},{25,17},{2,10},{10... | collective-permute-start | bytes 688136 | tf_op jit(solution)/shard_map/ppermute | solution.py:349
  268.1 3.5 %collective-permute-start = (s32[128]{0:T(128)S(1)}, s32[128]{0:T(128)S(1)}, u32[]{:S(2)}, u32[]{:S(2)}) collective-permute-start(s32[128]{0:T(128)S(1)} %reshape.353), channel_id=1, source_target_pairs={{0,16},{8,24},{16,0},{24,8},{1,17},{9,25},{17,1},{25,9},{2,18},{10... | collective-permute-start | bytes 1544 | tf_op jit(solution)/shard_map/ppermute | solution.py:346
  269.8 1.8 collective-permute-start.1
  271.6 1.1 collective-permute-start.2

commit v2 on v1

--- a/solution.py
+++ b/solution.py
@@ -408,13 +408,13 @@
         .reshape(3, TILE, slot_total * TILE)
     )
     margin = HALF
-    paired = jnp.stack([image_band, target[0]])
-    extended = with_halo(paired, (("wide", 2),), margin)
+    image_rows = with_halo(image_band, (("wide", 1),), margin)
+    target_rows = with_halo(target[0], (("wide", 1),), margin)
     loss_scale = 3.0 * view_total
     row_weight = jnp.ones((TILE,), jnp.float32)
     grad_rows = jax.grad(
-        lambda rows_now: structure_loss(rows_now, extended[1], TILE, row_weight, loss_scale)
-    )(extended[0])
+        lambda rows_now: structure_loss(rows_now, target_rows, TILE, row_weight, loss_scale)
+    )(image_rows)
     band_grad = grad_rows[:, HALF : HALF + TILE]
     rim_rows = jnp.concatenate([grad_rows[:, :HALF], grad_rows[:, HALF + TILE :]], axis=1)
     received = with_halo(rim_rows, (("wide", 1),), HALF)

time: 277 us -> 284 us (1.025); the launches traced: 275 us -> 286 us
  starting transfers between devices: 36.7 us -> 51 us
  waiting for transfers between devices: 54 us -> 45.3 us
  local copies, waits for them, and re-layouts: 25.9 us -> 30.4 us
    ppermute x2, starting transfers between devices: 3.02 us -> 12.9 us  [from_views(): lax.ppermute(values, 'view', [(i, (i + 2 * step) % views) for i in range(...]
    all_to_all x1, waiting for transfers between devices: 11.1 us -> 6.45 us  [on_device(): lax.all_to_all(sending, 'wide', split_axis=0, concat_axis=0, tiled=True)]
    ppermute x2 -> x3, starting transfers between devices: 7.07 us -> 10.3 us  [with_halo(): before = lax.ppermute(last, axis, up)]
    ppermute x2 -> x3, waiting for transfers between devices: 6.72 us -> 7.85 us  [with_halo(): after = lax.ppermute(leading, axis, down)]
  transfers between devices with their start and end apart: 14 -> 16, of which waited for: 10 -> 10; matrix products, arithmetic and copies ran while one was open for 3% -> 6% of each run, Pallas kernels for 0% -> 0%
where the time goes in v2:
time: 284 us; the launch traced here: 286 us
  Pallas kernels  105 us (37%)
  starting transfers between devices  51 us (18%)
  waiting for transfers between devices  45.3 us (16%)
  local copies, waits for them, and re-layouts  30.4 us (11%)
  other arithmetic  27.7 us (10%)
  blocking collectives  16.8 us (6%)
  between operations  8.78 us (3%)
    pallas_call x1, Pallas kernels, pull_tiles(): pl.pallas_call(pull_kernel, grid_spec=pltpu.PrefetchScalarGridSpec(num_sc...  65.7 us
    pallas_call x1, Pallas kernels, draw_tiles(): pl.pallas_call(functools.partial(draw_kernel, group), grid_spec=pltpu.Pre...  39.3 us
    all_to_all x1, blocking collectives, on_device(): lax.all_to_all(returning.reshape(wide_total, capacity, 8 * BLOCK)[:, :, :...  16.8 us
    all_to_all x1, waiting for transfers between devices, on_device(): lax.all_to_all(projected[asked], 'wide', split_axis=0, concat_axis=0, til...  13.7 us
    ppermute x2, starting transfers between devices, from_views(): lax.ppermute(values, 'view', [(i, (i + 2 * step) % views) for i in range(...  12.9 us
    ppermute x3, starting transfers between devices, with_halo(): before = lax.ppermute(last, axis, up)  10.3 us
    all_to_all x1, waiting for transfers between devices, on_device(): lax.all_to_all(by_slot, 'wide', split_axis=0, concat_axis=0, tiled=True)  9.12 us
    add x5, other arithmetic, blur_field(): across + tap_list[offset] * padded_input[:, :, offset:offset + field_width]  7.92 us
  transfers between devices with their start and end apart: 16, of which 10 were waited for; matrix products, arithmetic and copies ran while one was open for 6% of the time, Pallas kernels for 0%

profile of v2, /device:TPU:0, one launch (start us, length us, event | category | flops | bytes accessed | tf_op | source)
XLA Modules:
  0.0 285.6 jit_solution(2462380732786599873)
XLA Ops:
  4.1 7.3 %all-to-all-start = ((s32[8,1,20]{2,1,0:T(1,128)}), s32[8,1,20]{2,1,0:T(1,128)S(1)}, u32[]{:S(2)}, u32[]{:S(2)}) async-start(s32[8,1,20]{2,1,0:T(1,128)} %bitcast.13), calls=%async_computation | async-start | bytes 8192 | tf_op jit(solution)/shard_map/all_to_all | solution.py:378
  11.4 1.5 fusion.204
  16.6 1.4 copy.98
  18.1 1.9 add_dynamic-update-slice_fusion.1
  20.0 1.9 add_dynamic-update-slice_fusion
  28.5 1.5 gather_fusion
  30.0 6.0 %all-to-all-start.1 = ((f32[8,16,8,128]{3,2,1,0:T(8,128)}), f32[8,16,8,128]{3,2,1,0:T(8,128)S(1)}, u32[]{:S(2)}, u32[]{:S(2)}) async-start(f32[8,16,8,128]{3,2,1,0:T(8,128)} %bitcast.15), calls=%async_computation.1 | async-start | bytes 1048576 | tf_op jit(solution)/shard_map/all_to_all | solution.py:387
  36.3 13.7 %all-to-all-done.1 = f32[8,16,8,128]{3,2,1,0:T(8,128)S(1)} async-done(((f32[8,16,8,128]{3,2,1,0:T(8,128)}), f32[8,16,8,128]{3,2,1,0:T(8,128)S(1)}, u32[]{:S(2)}, u32[]{:S(2)}) %all-to-all-start.1) | async-done | bytes 524320 | tf_op jit(solution)/shard_map/all_to_all | solution.py:387
  50.8 39.3 %shard_map.77 = f32[32,3,1024]{2,1,0:T(4,128)S(1)} custom-call(s32[32]{0:T(128)S(1)} %reshape.344.lengths, s32[32]{0:T(128)S(1)} %reshape.345.cols, s32[32]{0:T(128)S(1)} %reshape.346.rows, f32[8]{0:T(128)S(1)} %concatenate.26.scalar_ref, f32[32,4,8,128]{3,2,1,0:T(8,128)S(1)} %bitcast.71, bf16[256,256]{1,0:T(8,128)(2,1)S(1)} %get-tuple-element.88.before_mat), custom_call_target="tpu_custom_call" | custom-call | tf_op jit(solution)/shard_map/pallas_call | solution.py:264
  90.0 1.0 copy.74
  91.0 6.5 %all-to-all-start.2 = ((f32[8,4,3,1024]{3,1,2,0:T(4,128)}), f32[8,4,3,1024]{3,1,2,0:T(4,128)S(1)}, u32[]{:S(2)}, u32[]{:S(2)}) async-start(f32[8,4,3,1024]{3,1,2,0:T(4,128)} %copy.74), calls=%async_computation.2 | async-start | bytes 786432 | tf_op jit(solution)/shard_map/all_to_all | solution.py:398
  97.6 3.9 %collective-permute-start.5 = (f32[3,5,1024]{2,1,0:T(8,128)S(1)}, f32[3,5,1024]{2,1,0:T(8,128)S(1)}, u32[]{:S(2)}, u32[]{:S(2)}) collective-permute-start(f32[3,5,1024]{2,1,0:T(8,128)S(1)} %get-tuple-element.83), channel_id=1, source_target_pairs={{0,1},{1,2},{2,3},{3,4},{4,5},{5,6},{6,7},{8,9},{9,10},{10,11},{11... | collective-permute-start | bytes 184328 | tf_op jit(solution)/shard_map/ppermute | solution.py:28
  101.5 1.3 collective-permute-start.6
  103.0 6.4 %all-to-all-done.2 = f32[8,4,3,1024]{3,1,2,0:T(4,128)S(1)} async-done(((f32[8,4,3,1024]{3,1,2,0:T(4,128)}), f32[8,4,3,1024]{3,1,2,0:T(4,128)S(1)}, u32[]{:S(2)}, u32[]{:S(2)}) %all-to-all-start.2) | async-done | bytes 393248 | tf_op jit(solution)/shard_map/all_to_all | solution.py:398
  110.9 1.7 reshape.355
  112.6 2.3 copy.77
  115.6 2.3 collective-permute-start.3
  118.0 1.5 collective-permute-start.4
  120.4 4.1 %collective-permute-done.4 = f32[3,5,1024]{2,1,0:T(8,128)S(1)} collective-permute-done((f32[3,5,1024]{2,1,0:T(8,128)S(1)}, f32[3,5,1024]{2,1,0:T(8,128)S(1)}, u32[]{:S(2)}, u32[]{:S(2)}) %collective-permute-start.4) | collective-permute-done | bytes 61472 | tf_op jit(solution)/shard_map/ppermute | solution.py:29
  124.7 1.6 fusion.98
  126.3 1.6 fusion.58
  127.9 1.6 fusion.18
  129.5 1.6 fusion.78
  131.1 1.6 fusion.38
  132.7 2.5 broadcast_multiply_fusion.18
  139.3 0.9 pad_add_fusion
  140.3 0.9 pad_add_fusion.1
  141.2 0.9 pad_add_fusion.2
  142.1 2.8 fusion.108
  145.0 4.0 %collective-permute-start.7 = (f32[3,5,1024]{2,1,0:T(8,128)S(1)}, f32[3,5,1024]{2,1,0:T(8,128)S(1)}, u32[]{:S(2)}, u32[]{:S(2)}) collective-permute-start(f32[3,5,1024]{2,1,0:T(8,128)S(1)} %get-tuple-element.43), channel_id=1, source_target_pairs={{0,1},{1,2},{2,3},{3,4},{4,5},{5,6},{6,7},{8,9},{9,10},{10,11},{11... | collective-permute-start | bytes 184328 | tf_op jit(solution)/shard_map/ppermute | solution.py:28
  149.0 1.3 collective-permute-start.8
  151.8 3.7 %collective-permute-done.8 = f32[3,5,1024]{2,1,0:T(8,128)S(1)} collective-permute-done((f32[3,5,1024]{2,1,0:T(8,128)S(1)}, f32[3,5,1024]{2,1,0:T(8,128)S(1)}, u32[]{:S(2)}, u32[]{:S(2)}) %collective-permute-start.8) | collective-permute-done | bytes 61472 | tf_op jit(solution)/shard_map/ppermute | solution.py:29
  155.8 1.7 reshape.358
  157.5 3.5 %copy.96 = f32[3,32,32,32]{3,1,2,0:T(8,128)} copy(f32[3,32,32,32]{3,2,1,0:T(8,128)} %reshape.358) | data formatting | bytes 786432 | tf_op jit(solution)/shard_map/reshape | solution.py:428
  161.0 2.1 reshape.359
  163.4 1.0 gather_fusion.3
  164.4 1.0 copy.81
  165.4 3.7 %all-to-all-start.3 = ((f32[8,4,3,1024]{3,1,2,0:T(4,128)}), f32[8,4,3,1024]{3,1,2,0:T(4,128)S(1)}, u32[]{:S(2)}, u32[]{:S(2)}) async-start(f32[8,4,3,1024]{3,1,2,0:T(4,128)} %copy.81), calls=%async_computation.3 | async-start | bytes 786432 | tf_op jit(solution)/shard_map/all_to_all | solution.py:435
  169.2 9.1 %all-to-all-done.3 = f32[8,4,3,1024]{3,1,2,0:T(4,128)S(1)} async-done(((f32[8,4,3,1024]{3,1,2,0:T(4,128)}), f32[8,4,3,1024]{3,1,2,0:T(4,128)S(1)}, u32[]{:S(2)}, u32[]{:S(2)}) %all-to-all-start.3) | async-done | bytes 393248 | tf_op jit(solution)/shard_map/all_to_all | solution.py:435
  179.3 65.7 %shard_map.78 = f32[32,4,8,128]{3,2,1,0:T(8,128)S(1)} custom-call(s32[32]{0:T(128)S(1)} %reshape.344.lengths, s32[32]{0:T(128)S(1)} %reshape.345.cols, s32[32]{0:T(128)S(1)} %reshape.346.rows, f32[8]{0:T(128)S(1)} %concatenate.26.scalar_ref, f32[32,4,8,128]{3,2,1,0:T(8,128)S(1)} %bitcast.72, bf16[32,16,1024]{2,1,0:T(8,128)(2,1)S(1)} %maximum_maximum_fusion.grads, ...), custom_call_target="tpu_custom_call" | custom-call | tf_op jit(solution)/shard_map/pallas_call | solution.py:285
  245.3 16.8 %all_to_all.32 = bf16[8,16,896]{2,1,0:T(8,128)(2,1)S(1)} all-to-all(bf16[8,16,896]{2,1,0:T(8,128)(2,1)S(1)} %slice.669), channel_id=1, replica_groups=mesh['view'=4,'wide'=8] {'wide'}, dimensions={0} | all-to-all | bytes 458752 | tf_op jit(solution)/shard_map/all_to_all | solution.py:448
  262.1 10.9 %collective-permute-start.9 = (bf16[128,896]{1,0:T(8,128)(2,1)S(1)}, bf16[128,896]{1,0:T(8,128)(2,1)S(1)}, u32[]{:S(2)}, u32[]{:S(2)}) collective-permute-start(bf16[128,896]{1,0:T(8,128)(2,1)S(1)} %bitcast.94), channel_id=1, source_target_pairs={{0,16},{8,24},{16,0},{24,8},{1,17},{9,25},{17,1},{25,9},{2,18},{10... | collective-permute-start | bytes 688136 | tf_op jit(solution)/shard_map/ppermute | solution.py:346
  273.0 4.0 %collective-permute-done.9 = bf16[128,896]{1,0:T(8,128)(2,1)S(1)} collective-permute-done((bf16[128,896]{1,0:T(8,128)(2,1)S(1)}, bf16[128,896]{1,0:T(8,128)(2,1)S(1)}, u32[]{:S(2)}, u32[]{:S(2)}) %collective-permute-start.9) | collective-permute-done | bytes 229408 | tf_op jit(solution)/shard_map/ppermute | solution.py:346
  277.1 2.0 collective-permute-start
  279.4 1.3 collective-permute-done
  280.7 1.1 collective-permute-done.2
  281.8 1.5 broadcast_in_dim_reshape.4
  284.1 1.5 copy.97
  (102 shorter events, 19.2 us)
Async XLA Ops:
  2.8 0.5 copy-start.5
  4.1 22.9 %all-to-all-start = ((s32[8,1,20]{2,1,0:T(1,128)}), s32[8,1,20]{2,1,0:T(1,128)S(1)}, u32[]{:S(2)}, u32[]{:S(2)}) async-start(s32[8,1,20]{2,1,0:T(1,128)} %bitcast.13), calls=%async_computation | async-start | bytes 8192 | tf_op jit(solution)/shard_map/all_to_all | solution.py:378
  18.0 7.8 %copy-start.3 = (s32[1,8,4]{1,2,0:T(4,128)S(1)}, s32[1,8,4]{1,2,0:T(4,128)}, u32[]{:S(2)}) copy-start(s32[1,8,4]{1,2,0:T(4,128)} %param.12) | copy-start | bytes 388
  18.1 8.0 %copy-start.4 = (s32[1,8,4]{1,2,0:T(4,128)S(1)}, s32[1,8,4]{1,2,0:T(4,128)}, u32[]{:S(2)}) copy-start(s32[1,8,4]{1,2,0:T(4,128)} %param.14) | copy-start | bytes 388
  27.0 9.0 %copy-start.1 = (f32[1,6]{1,0:T(1,128)S(1)}, f32[1,6]{1,0:T(1,128)}, u32[]{:S(2)}) copy-start(f32[1,6]{1,0:T(1,128)} %param.11) | copy-start | bytes 76
  30.0 20.0 %all-to-all-start.1 = ((f32[8,16,8,128]{3,2,1,0:T(8,128)}), f32[8,16,8,128]{3,2,1,0:T(8,128)S(1)}, u32[]{:S(2)}, u32[]{:S(2)}) async-start(f32[8,16,8,128]{3,2,1,0:T(8,128)} %bitcast.15), calls=%async_computation.1 | async-start | bytes 1048576 | tf_op jit(solution)/shard_map/all_to_all | solution.py:387
  50.8 46.8 %copy-start = (f32[1,3,32,1024]{3,2,1,0:T(8,128)S(1)}, f32[1,3,32,1024]{3,2,1,0:T(8,128)}, u32[]{:S(2)}) copy-start(f32[1,3,32,1024]{3,2,1,0:T(8,128)} %param.15) | copy-start | bytes 1179652
  91.0 18.4 %all-to-all-start.2 = ((f32[8,4,3,1024]{3,1,2,0:T(4,128)}), f32[8,4,3,1024]{3,1,2,0:T(4,128)S(1)}, u32[]{:S(2)}, u32[]{:S(2)}) async-start(f32[8,4,3,1024]{3,1,2,0:T(4,128)} %copy.74), calls=%async_computation.2 | async-start | bytes 786432 | tf_op jit(solution)/shard_map/all_to_all | solution.py:398
  97.6 21.8 %collective-permute-start.5 = (f32[3,5,1024]{2,1,0:T(8,128)S(1)}, f32[3,5,1024]{2,1,0:T(8,128)S(1)}, u32[]{:S(2)}, u32[]{:S(2)}) collective-permute-start(f32[3,5,1024]{2,1,0:T(8,128)S(1)} %get-tuple-element.83), channel_id=1, source_target_pairs={{0,1},{1,2},{2,3},{3,4},{4,5},{5,6},{6,7},{8,9},{9,10},{10,11},{11... | collective-permute-start | bytes 184328 | tf_op jit(solution)/shard_map/ppermute | solution.py:28
  101.5 17.9 %collective-permute-start.6 = (f32[3,5,1024]{2,1,0:T(8,128)S(1)}, f32[3,5,1024]{2,1,0:T(8,128)S(1)}, u32[]{:S(2)}, u32[]{:S(2)}) collective-permute-start(f32[3,5,1024]{2,1,0:T(8,128)S(1)} %get-tuple-element.84), channel_id=1, source_target_pairs={{1,0},{2,1},{3,2},{4,3},{5,4},{6,5},{7,6},{9,8},{10,9},{11,10},{12... | collective-permute-start | bytes 184328 | tf_op jit(solution)/shard_map/ppermute | solution.py:29
  115.6 4.7 %collective-permute-start.3 = (f32[3,5,1024]{2,1,0:T(8,128)S(1)}, f32[3,5,1024]{2,1,0:T(8,128)S(1)}, u32[]{:S(2)}, u32[]{:S(2)}) collective-permute-start(f32[3,5,1024]{2,1,0:T(8,128)S(1)} %get-tuple-element.81), channel_id=1, source_target_pairs={{0,1},{1,2},{2,3},{3,4},{4,5},{5,6},{6,7},{8,9},{9,10},{10,11},{11... | collective-permute-start | bytes 184328 | tf_op jit(solution)/shard_map/ppermute | solution.py:28
  118.0 6.5 %collective-permute-start.4 = (f32[3,5,1024]{2,1,0:T(8,128)S(1)}, f32[3,5,1024]{2,1,0:T(8,128)S(1)}, u32[]{:S(2)}, u32[]{:S(2)}) collective-permute-start(f32[3,5,1024]{2,1,0:T(8,128)S(1)} %get-tuple-element.82), channel_id=1, source_target_pairs={{1,0},{2,1},{3,2},{4,3},{5,4},{6,5},{7,6},{9,8},{10,9},{11,10},{12... | collective-permute-start | bytes 184328 | tf_op jit(solution)/shard_map/ppermute | solution.py:29
  145.0 6.2 %collective-permute-start.7 = (f32[3,5,1024]{2,1,0:T(8,128)S(1)}, f32[3,5,1024]{2,1,0:T(8,128)S(1)}, u32[]{:S(2)}, u32[]{:S(2)}) collective-permute-start(f32[3,5,1024]{2,1,0:T(8,128)S(1)} %get-tuple-element.43), channel_id=1, source_target_pairs={{0,1},{1,2},{2,3},{3,4},{4,5},{5,6},{6,7},{8,9},{9,10},{10,11},{11... | collective-permute-start | bytes 184328 | tf_op jit(solution)/shard_map/ppermute | solution.py:28
  149.0 6.5 %collective-permute-start.8 = (f32[3,5,1024]{2,1,0:T(8,128)S(1)}, f32[3,5,1024]{2,1,0:T(8,128)S(1)}, u32[]{:S(2)}, u32[]{:S(2)}) collective-permute-start(f32[3,5,1024]{2,1,0:T(8,128)S(1)} %get-tuple-element.42), channel_id=1, source_target_pairs={{1,0},{2,1},{3,2},{4,3},{5,4},{6,5},{7,6},{9,8},{10,9},{11,10},{12... | collective-permute-start | bytes 184328 | tf_op jit(solution)/shard_map/ppermute | solution.py:29
  165.4 12.9 %all-to-all-start.3 = ((f32[8,4,3,1024]{3,1,2,0:T(4,128)}), f32[8,4,3,1024]{3,1,2,0:T(4,128)S(1)}, u32[]{:S(2)}, u32[]{:S(2)}) async-start(f32[8,4,3,1024]{3,1,2,0:T(4,128)} %copy.81), calls=%async_computation.3 | async-start | bytes 786432 | tf_op jit(solution)/shard_map/all_to_all | solution.py:435
  179.3 65.7 %copy-start.6 = (s32[128]{0:T(128)S(1)}, s32[128]{0:T(128)}, u32[]{:S(2)}) copy-start(s32[128]{0:T(128)} %copy-done.5) | copy-start | bytes 1540
  245.0 32.1 %copy-start.2 = (s32[8,16]{1,0:T(8,128)S(1)}, s32[8,16]{1,0:T(8,128)}, u32[]{:S(2)}) copy-start(s32[8,16]{1,0:T(8,128)} %get-tuple-element.85) | copy-start | bytes 1540
  262.1 14.9 %collective-permute-start.9 = (bf16[128,896]{1,0:T(8,128)(2,1)S(1)}, bf16[128,896]{1,0:T(8,128)(2,1)S(1)}, u32[]{:S(2)}, u32[]{:S(2)}) collective-permute-start(bf16[128,896]{1,0:T(8,128)(2,1)S(1)} %bitcast.94), channel_id=1, source_target_pairs={{0,16},{8,24},{16,0},{24,8},{1,17},{9,25},{17,1},{25,9},{2,18},{10... | collective-permute-start | bytes 688136 | tf_op jit(solution)/shard_map/ppermute | solution.py:346
  273.0 10.2 %collective-permute-start.10 = (bf16[128,896]{1,0:T(8,128)(2,1)S(1)}, bf16[128,896]{1,0:T(8,128)(2,1)S(1)}, u32[]{:S(2)}, u32[]{:S(2)}) collective-permute-start(bf16[128,896]{1,0:T(8,128)(2,1)S(1)} %bitcast.95), channel_id=1, source_target_pairs={{0,8},{8,0},{16,24},{24,16},{1,9},{9,1},{17,25},{25,17},{2,10},{10... | collective-permute-start | bytes 688136 | tf_op jit(solution)/shard_map/ppermute | solution.py:349
  277.0 6.2 %collective-permute-start.11 = (bf16[128,896]{1,0:T(8,128)(2,1)S(1)}, bf16[128,896]{1,0:T(8,128)(2,1)S(1)}, u32[]{:S(2)}, u32[]{:S(2)}) collective-permute-start(bf16[128,896]{1,0:T(8,128)(2,1)S(1)} %collective-permute-done.9), channel_id=1, source_target_pairs={{0,8},{8,0},{16,24},{24,16},{1,9},{9,1},{17,25},{25,17},{2,10},{10... | collective-permute-start | bytes 688136 | tf_op jit(solution)/shard_map/ppermute | solution.py:349
  277.1 3.5 %collective-permute-start = (s32[128]{0:T(128)S(1)}, s32[128]{0:T(128)S(1)}, u32[]{:S(2)}, u32[]{:S(2)}) collective-permute-start(s32[128]{0:T(128)S(1)} %reshape.356), channel_id=1, source_target_pairs={{0,16},{8,24},{16,0},{24,8},{1,17},{9,25},{17,1},{25,9},{2,18},{10... | collective-permute-start | bytes 1544 | tf_op jit(solution)/shard_map/ppermute | solution.py:346
  279.1 1.5 collective-permute-start.1
  280.6 1.1 collective-permute-start.2
